TPU v7x, 32 devices: a whole 2x2x4 slice. The times are simulated.
32 devices in a mesh: mp: 2 (over y), gx: 8 (over z, x), gy: 2 (over core).
Axes of the slice: x: 2, y: 2, z: 4, core: 2. Of those that a mesh axis runs over, the one named last changes fastest.
Arguments:
- tracers: float32 [16, 60, 128, 512], P(None, None, 'gx', ('mp', 'gy')), may hold values from -6 to 6
- wind_courant: float32 [2, 60, 128, 512], P(None, None, 'gx', ('mp', 'gy')), may hold values from -0.45 to 0.45
- pressure_head: float32 [8, 128, 512], P(None, ('gx', 'gy'), 'mp'), may hold values from -2 to 0.5
- storage: float32 [8, 128, 512], P(None, ('gx', 'gy'), 'mp'), may hold values from 0.05 to 0.5
- soil_type: int32 [128, 512], P(('gx', 'gy'), 'mp'), may hold values from 0 to 11
- land_mask: int32 [128, 512], P(('gx', 'gy'), 'mp'), may hold values 0 or 1
- conductivity_table: float32 [12], replicated, may hold values from 0.3 to 3
- exponent_table: float32 [12], replicated, may hold values from 0.2 to 1
Outputs:
- tracers_out: float32 [16, 60, 128, 512], P(None, None, 'gx', ('mp', 'gy'))
- new_head: float32 [8, 128, 512], P(None, ('gx', 'gy'), 'mp')
All inputs are finite; a program needn't handle non-finite values. No bound on the sum of `land_mask` on one device may be relied on, other than what follows from the above.
Results may differ from a plain program's by a relative error of at most 0.00002.
Values sent between devices are 32-bit elements; how exact they have to be, the bound alone decides.
A program may use at most 256 MiB of HBM per device.

v0:
```python
import functools

import jax
import jax.numpy as jnp
from jax import lax
from jax.experimental import pallas as pl
from jax.experimental.pallas import tpu as pltpu
from jax.sharding import PartitionSpec as P

SWEEPS = 3
MESH = pl.DeviceIdType.MESH
UP, DOWN, RIGHT, LEFT = range(4)


def softplus(value):
    return jnp.maximum(value, 0.0) + jnp.log(1.0 + jnp.exp(-jnp.abs(value)))


def harmonic(first_cond, second_cond):
    summed = first_cond + second_cond
    return 2.0 * first_cond * second_cond / jnp.where(summed > 0.0, summed, 1.0)


def kernel(
    sizes,
    tracers_hbm,
    wind_hbm,
    head_hbm,
    storage_hbm,
    type_hbm,
    mask_hbm,
    cond_table,
    exp_table,
    out_hbm,
    head_out_hbm,
    q,
    wind,
    row_send,
    row_recv,
    col_send,
    col_recv,
    head,
    storage,
    soil_type,
    mask,
    saturated,
    exponent,
    iterate,
    cond,
    surface_send,
    surface,
    edge_send,
    edge_recv,
    side_send,
    side_recv,
    load_sem,
    soil_sem,
    store_sem,
    send_sem,
    recv_sem,
    edge_send_sem,
    edge_recv_sem,
    surface_sem,
    head_sem,
):
    n_mp, n_gx, n_gy, chunk = sizes
    species, levels, rows, cols = tracers_hbm.shape
    layers, soil_rows, soil_cols = head_hbm.shape
    chunks = levels // chunk
    mp, gx, gy = lax.axis_index("mp"), lax.axis_index("gx"), lax.axis_index("gy")
    across = mp * n_gy + gy
    along = gx * n_gy + gy
    n_across, n_along = n_mp * n_gy, n_gx * n_gy

    def across_device(index):
        return (index // n_gy, gx, lax.rem(index, n_gy))

    def along_device(index):
        return (mp, index // n_gy, lax.rem(index, n_gy))

    sends = (gx < n_gx - 1, gx > 0, across < n_across - 1, across > 0)
    gets = (gx > 0, gx < n_gx - 1, across > 0, across < n_across - 1)
    targets = (
        (mp, gx + 1, gy),
        (mp, gx - 1, gy),
        across_device(across + 1),
        across_device(across - 1),
    )

    def load(c):
        part = pl.ds(c * chunk, chunk)
        return (
            pltpu.make_async_copy(wind_hbm.at[:, part], wind.at[:, part], load_sem.at[0, c]),
            pltpu.make_async_copy(tracers_hbm.at[:, part], q.at[:, part], load_sem.at[1, c]),
        )

    def store(c):
        part = pl.ds(c * chunk, chunk)
        return pltpu.make_async_copy(q.at[:, part], out_hbm.at[:, part], store_sem.at[c])

    @pl.loop(0, chunks)
    def _(c):
        for copy in load(c):
            copy.start()

    soil_loads = [
        pltpu.make_async_copy(source, target, soil_sem.at[place])
        for place, (source, target) in enumerate(
            ((head_hbm, head), (storage_hbm, storage), (type_hbm, soil_type), (mask_hbm, mask))
        )
    ]
    for copy in soil_loads:
        copy.start()

    barrier = pltpu.get_barrier_semaphore()
    other_chip = lax.rem(mp + 1, n_mp)
    greeted = list(zip(sends, targets)) + [
        (jnp.logical_and(along > 0, gy == 0), along_device(along - 1)),
        (jnp.logical_and(along < n_along - 1, gy == n_gy - 1), along_device(along + 1)),
        (mp >= 0, (other_chip, gx, gy)),
    ]
    for there, device in greeted:

        @pl.when(there)
        def _(device=device):
            pl.semaphore_signal(barrier, inc=1, device_id=device, device_id_type=MESH)

    pl.semaphore_wait(barrier, sum(there.astype(jnp.int32) for there, _ in greeted))

    for way in range(4):
        place = row_recv if way < 2 else col_recv

        @pl.when(jnp.logical_not(gets[way]))
        def _(place=place, way=way):
            place[:, way % 2] = jnp.zeros_like(place[:, way % 2])

    def transfer(c, turn, way):
        part = pl.ds(c * chunk, chunk)
        source, target = (row_send, row_recv) if way < 2 else (col_send, col_recv)
        return pltpu.make_async_remote_copy(
            src_ref=source.at[turn, way % 2, part],
            dst_ref=target.at[turn, way % 2, part],
            send_sem=send_sem.at[turn, way, c],
            recv_sem=recv_sem.at[turn, way, c],
            device_id=targets[way],
            device_id_type=MESH,
        )

    def start(c, turn):
        for way in range(4):

            @pl.when(sends[way])
            def _(way=way):
                transfer(c, turn, way).start()

    def arrive(c, turn):
        for way in range(4):

            @pl.when(gets[way])
            def _(way=way):
                transfer(c, turn, way).wait_recv()

    lane = lax.broadcasted_iota(jnp.int32, (rows, cols), 1)
    row = lax.broadcasted_iota(jnp.int32, (rows, cols), 0)

    def winds(level):
        u, v = wind[0, level], wind[1, level]
        return jnp.maximum(u, 0.0), jnp.minimum(u, 0.0), jnp.maximum(v, 0.0), jnp.minimum(v, 0.0)

    def pack(level, turn, kind, field, parts, packed):
        u_pos, u_neg, v_pos, v_neg = parts
        right, left = packed
        row_send[turn, UP, level, kind : kind + 1] = (u_pos * field)[rows - 1 : rows]
        row_send[turn, DOWN, level, kind : kind + 1] = (u_neg * field)[0:1]
        right = jnp.where(
            lane == kind, pltpu.roll(v_pos * field, (kind + 1) % cols, 1), right
        )
        left_part = v_neg * field
        if kind > 0:
            left_part = pltpu.roll(left_part, kind, 1)
        left = jnp.where(lane == kind, left_part, left)
        return right, left

    def pack_done(level, turn, packed):
        col_send[turn, 0, level] = packed[0]
        col_send[turn, 1, level] = packed[1]

    def blank():
        return (jnp.zeros((rows, cols), jnp.float32),) * 2

    def advance(level, turn, kind, parts):
        u_pos, u_neg, v_pos, v_neg = parts
        field = q[kind, level]
        plus, minus = u_pos * field, u_neg * field
        above = row_recv[turn, DOWN, level, kind : kind + 1]
        below = row_recv[turn, UP, level, kind : kind + 1]
        face = plus + jnp.where(row == rows - 1, above, pltpu.roll(minus, rows - 1, 0))
        face_before = jnp.where(row == 0, below + minus, pltpu.roll(face, 1, 0))
        plus, minus = v_pos * field, v_neg * field
        from_left = col_recv[turn, 0, level]
        if kind > 0:
            from_left = pltpu.roll(from_left, cols - kind, 1)
        from_right = pltpu.roll(col_recv[turn, 1, level], cols - 1 - kind, 1)
        side = plus + jnp.where(lane == cols - 1, from_right, pltpu.roll(minus, cols - 1, 1))
        side_before = jnp.where(lane == 0, from_left, pltpu.roll(plus, 1, 1)) + minus
        return field - (face - face_before) - (side - side_before)

    def first_edges(c):
        @pl.loop(c * chunk, (c + 1) * chunk)
        def _(level):
            parts, packed = winds(level), blank()
            for kind in range(species):
                packed = pack(level, 0, kind, q[kind, level], parts, packed)
            pack_done(level, 0, packed)

    def first_step(c):
        @pl.loop(c * chunk, (c + 1) * chunk)
        def _(level):
            parts, packed = winds(level), blank()
            for kind in range(species):
                field = advance(level, 0, kind, parts)
                packed = pack(level, 1, kind, field, parts, packed)
                q[kind, level] = field
            pack_done(level, 1, packed)

    def second_step(c):
        @pl.loop(c * chunk, (c + 1) * chunk)
        def _(level):
            parts = winds(level)
            for kind in range(species):
                q[kind, level] = advance(level, 1, kind, parts)

    edge_sends = (along < n_along - 1, along > 0, mp >= 0)
    edge_gets = (along > 0, along < n_along - 1, mp >= 0)
    edge_targets = (along_device(along + 1), along_device(along - 1), (other_chip, gx, gy))
    half = soil_cols // 2

    def edge_transfer(turn, way):
        source, target = (
            (edge_send.at[turn, way], edge_recv.at[turn, way])
            if way < 2
            else (side_send.at[turn], side_recv.at[turn])
        )
        return pltpu.make_async_remote_copy(
            src_ref=source,
            dst_ref=target,
            send_sem=edge_send_sem.at[turn, way],
            recv_sem=edge_recv_sem.at[turn, way],
            device_id=edge_targets[way],
            device_id_type=MESH,
        )

    def soil_edges(turn):
        for layer in range(layers):
            values = iterate[layer]
            conds = saturated[...] * jnp.exp(exponent[...] * jnp.minimum(values, 0.0))
            cond[layer] = conds
            for place, array in enumerate((values, conds)):
                edge_send[turn, 0, place, layer : layer + 1] = array[soil_rows - 1 : soil_rows]
                edge_send[turn, 1, place, layer : layer + 1] = array[0:1]
                side_send[turn, place, layer] = jnp.where(mp == 0, array[:, half:], array[:, :half])
        for way in range(3):

            @pl.when(edge_sends[way])
            def _(way=way):
                edge_transfer(turn, way).start()

    soil_row = lax.broadcasted_iota(jnp.int32, (soil_rows, soil_cols), 0)
    soil_lane = lax.broadcasted_iota(jnp.int32, (soil_rows, soil_cols), 1)

    def soil_sweep(turn):
        for way in range(3):

            @pl.when(edge_gets[way])
            def _(way=way):
                edge_transfer(turn, way).wait_recv()

        def neighbours(place, layer, array):
            low = edge_recv[turn, 0, place, layer : layer + 1]
            high = edge_recv[turn, 1, place, layer : layer + 1]
            side = side_recv[turn, place, layer]
            side = jnp.concatenate([side, side], axis=1)
            left_end = jnp.where(mp == 0, 0.0, pltpu.roll(side, 1, 1))
            right_end = jnp.where(mp == n_mp - 1, 0.0, pltpu.roll(side, soil_cols - 1, 1))
            return (
                jnp.where(soil_row == 0, low, pltpu.roll(array, 1, 0)),
                jnp.where(soil_row == soil_rows - 1, high, pltpu.roll(array, soil_rows - 1, 0)),
                jnp.where(soil_lane == 0, left_end, pltpu.roll(array, 1, 1)),
                jnp.where(soil_lane == soil_cols - 1, right_end, pltpu.roll(array, soil_cols - 1, 1)),
            )

        values = [iterate[layer] for layer in range(layers)]
        below_faces = [harmonic(cond[i], cond[i + 1]) for i in range(layers - 1)]
        for layer in range(layers):
            center = cond[layer]
            capacity = storage[layer]
            top, bottom = capacity * head[layer], capacity
            for near_cond, near in zip(
                neighbours(1, layer, center), neighbours(0, layer, values[layer])
            ):
                face = harmonic(center, near_cond)
                top = top + face * near
                bottom = bottom + face
            if layer > 0:
                face = below_faces[layer - 1]
                top = top + face * values[layer - 1] + face
                bottom = bottom + face
            if layer < layers - 1:
                face = below_faces[layer]
                top = top + face * values[layer + 1] - face
                bottom = bottom + face
            if layer == 0:
                top = top + mask[...].astype(jnp.float32) * surface[...]
            if layer == layers - 1:
                top = top - center
            iterate[layer] = top / bottom

    def soil_start():
        for copy in soil_loads:
            copy.wait()
        kinds = soil_type[...]
        for target, table in ((saturated, cond_table), (exponent, exp_table)):
            found = jnp.zeros(kinds.shape, jnp.float32)
            for kind in range(table.shape[0]):
                found = jnp.where(kinds == kind, table[kind], found)
            target[...] = found
        for way in range(2):

            @pl.when(jnp.logical_not(edge_gets[way]))
            def _(way=way):
                edge_recv[:, way] = jnp.zeros_like(edge_recv[:, way])

        iterate[...] = head[...]
        soil_edges(0)

    def surface_transfer(core):
        return pltpu.make_async_remote_copy(
            src_ref=surface_send,
            dst_ref=surface.at[:, pl.ds(core * cols, cols)],
            send_sem=surface_sem.at[0],
            recv_sem=surface_sem.at[1],
            device_id=(mp, gx, 1 - gy),
            device_id_type=MESH,
        )

    def surface_start():
        precip = softplus(q[3, 0])
        evaporation = softplus(-q[1, 0])
        radiation = jnp.exp(-softplus(q[2, 0])) / (1.0 + jnp.exp(-q[0, 0]))
        field = precip - evaporation * radiation
        for core in range(2):

            @pl.when(gy == core)
            def _(core=core):
                other = 1 - core
                surface[:, core * cols : (core + 1) * cols] = field[
                    core * soil_rows : (core + 1) * soil_rows
                ]
                surface_send[...] = field[other * soil_rows : (other + 1) * soil_rows]
                surface_transfer(core).start()

    def surface_wait():
        for core in range(2):

            @pl.when(gy == core)
            def _(core=core):
                surface_transfer(1 - core).wait_recv()
                surface_transfer(core).wait_send()

    head_store = pltpu.make_async_copy(iterate, head_out_hbm, head_sem.at[0])

    @pl.loop(0, chunks + 2)
    def _(turn):
        @pl.when(turn < chunks)
        def _():
            for copy in load(turn):
                copy.wait()
            first_edges(turn)
            start(turn, 0)

        @pl.when(turn == 0)
        def _():
            soil_start()

        @pl.when(jnp.logical_and(turn >= 1, turn <= chunks))
        def _():
            arrive(turn - 1, 0)
            first_step(turn - 1)
            start(turn - 1, 1)

        @pl.when(turn >= 2)
        def _():
            arrive(turn - 2, 1)
            second_step(turn - 2)
            store(turn - 2).start()

        @pl.when(turn == 2)
        def _():
            surface_start()

        @pl.when(turn == 4)
        def _():
            surface_wait()
            soil_sweep(0)
            soil_edges(1)

        @pl.when(turn == 6)
        def _():
            soil_sweep(1)
            soil_edges(2)

        @pl.when(turn == 8)
        def _():
            soil_sweep(2)
            head_store.start()

    for turn in range(SWEEPS):
        for way in range(3):

            @pl.when(edge_sends[way])
            def _(turn=turn, way=way):
                edge_transfer(turn, way).wait_send()

    head_store.wait()

    @pl.loop(0, chunks)
    def _(c):
        for turn in range(2):
            for way in range(4):

                @pl.when(sends[way])
                def _(turn=turn, way=way):
                    transfer(c, turn, way).wait_send()

        store(c).wait()


def on_device(sizes, *arguments):
    tracers, wind, head = arguments[:3]
    species, levels, rows, cols = tracers.shape
    layers, soil_rows, soil_cols = head.shape
    chunk = next(c for c in (6, 5, 4, 3, 2, 1) if levels % c == 0)
    chunks = levels // chunk
    f32 = jnp.float32
    anywhere = pl.BlockSpec(memory_space=pl.ANY)
    scalars = pl.BlockSpec(memory_space=pltpu.SMEM)
    soil = (layers, soil_rows, soil_cols)
    return pl.pallas_call(
        functools.partial(kernel, sizes + (chunk,)),
        out_shape=(
            jax.ShapeDtypeStruct(tracers.shape, f32),
            jax.ShapeDtypeStruct(head.shape, f32),
        ),
        in_specs=[pl.BlockSpec(memory_space=pltpu.HBM)] * 6 + [scalars] * 2,
        out_specs=(anywhere, anywhere),
        scratch_shapes=[
            pltpu.VMEM(tracers.shape, f32),
            pltpu.VMEM(wind.shape, f32),
            pltpu.VMEM((2, 2, levels, species, cols), f32),
            pltpu.VMEM((2, 2, levels, species, cols), f32),
            pltpu.VMEM((2, 2, levels, rows, cols), f32),
            pltpu.VMEM((2, 2, levels, rows, cols), f32),
            pltpu.VMEM(soil, f32),
            pltpu.VMEM(soil, f32),
            pltpu.VMEM(soil[1:], jnp.int32),
            pltpu.VMEM(soil[1:], jnp.int32),
            pltpu.VMEM(soil[1:], f32),
            pltpu.VMEM(soil[1:], f32),
            pltpu.VMEM(soil, f32),
            pltpu.VMEM(soil, f32),
            pltpu.VMEM((soil_rows, cols), f32),
            pltpu.VMEM((soil_rows, soil_cols), f32),
            pltpu.VMEM((SWEEPS, 2, 2, layers, soil_cols), f32),
            pltpu.VMEM((SWEEPS, 2, 2, layers, soil_cols), f32),
            pltpu.VMEM((SWEEPS, 2, layers, soil_rows, soil_cols // 2), f32),
            pltpu.VMEM((SWEEPS, 2, layers, soil_rows, soil_cols // 2), f32),
            pltpu.SemaphoreType.DMA((2, chunks)),
            pltpu.SemaphoreType.DMA((4,)),
            pltpu.SemaphoreType.DMA((chunks,)),
            pltpu.SemaphoreType.DMA((2, 4, chunks)),
            pltpu.SemaphoreType.DMA((2, 4, chunks)),
            pltpu.SemaphoreType.DMA((SWEEPS, 3)),
            pltpu.SemaphoreType.DMA((SWEEPS, 3)),
            pltpu.SemaphoreType.DMA((2,)),
            pltpu.SemaphoreType.DMA((1,)),
        ],
        compiler_params=pltpu.CompilerParams(
            collective_id=0, has_side_effects=True, vmem_limit_bytes=28 * 1024 * 1024
        ),
    )(*arguments)


def solution(mesh):
    tall, flat = P(None, None, "gx", ("mp", "gy")), P(None, ("gx", "gy"), "mp")
    ground = P(("gx", "gy"), "mp")
    sizes = (mesh.shape["mp"], mesh.shape["gx"], mesh.shape["gy"])
    return jax.shard_map(
        functools.partial(on_device, sizes),
        mesh=mesh,
        in_specs=(tall, tall, flat, flat, ground, ground, P(), P()),
        out_specs=(tall, flat),
        check_vma=False,
    )
```

profile of v0, /device:TPU:16, one launch (start us, length us, event | category | flops | bytes accessed | tf_op | source)
XLA Modules:
  0.0 88.3 jit_solution(11395859998987545002)
XLA Ops:
  0.6 0.0 copy-start
  0.6 3.2 %copy-done = f32[16,60,16,128]{3,2,1,0:T(8,128)S(1)} copy-done((f32[16,60,16,128]{3,2,1,0:T(8,128)S(1)}, f32[16,60,16,128]{3,2,1,0:T(8,128)}, u32[]{:S(2)}) %copy-start) | copy-done | bytes 7864344
  3.9 0.0 copy-start.1
  3.9 1.2 %copy-done.1 = f32[2,60,16,128]{3,2,1,0:T(8,128)S(1)} copy-done((f32[2,60,16,128]{3,2,1,0:T(8,128)S(1)}, f32[2,60,16,128]{3,2,1,0:T(8,128)}, u32[]{:S(2)}) %copy-start.1) | copy-done | bytes 983064
  5.1 0.0 copy-start.2
  5.1 0.8 copy-done.2
  5.9 0.0 copy-start.3
  5.9 0.8 copy-done.3
  6.7 0.0 copy-start.4
  6.8 0.7 copy-done.4
  7.4 0.0 copy-start.5
  7.4 0.7 copy-done.5
  8.1 0.0 copy-start.6
  8.1 0.7 copy-done.6
  8.8 0.0 copy-start.7
  8.8 0.7 copy-done.7
  9.5 75.0 %shard_map.95 = (f32[16,60,16,128]{3,2,1,0:T(8,128)S(1)}, f32[8,8,256]{2,1,0:T(8,128)S(1)}) custom-call(f32[16,60,16,128]{3,2,1,0:T(8,128)S(1)} %copy-done, f32[2,60,16,128]{3,2,1,0:T(8,128)S(1)} %copy-done.1, f32[8,8,256]{2,1,0:T(8,128)S(1)} %copy-done.2, f32[8,8,256]{2,1,0:T(8,128)S(1)} %copy-done.3, s32[8,256]{1,0:T(8,128)S(1)} %copy-done.4, ...), custom_call_target="tpu_custom_call" | custom-call | tf_op jit(solution)/shard_map/pallas_call | solution.py:448
  84.4 3.2 %copy.12 = f32[16,60,16,128]{3,2,1,0:T(8,128)} copy(f32[16,60,16,128]{3,2,1,0:T(8,128)S(1)} %get-tuple-element.4) | data formatting | bytes 15728640
  87.7 0.6 copy.13
Async XLA Ops:
  0.6 3.2 %copy-start = (f32[16,60,16,128]{3,2,1,0:T(8,128)S(1)}, f32[16,60,16,128]{3,2,1,0:T(8,128)}, u32[]{:S(2)}) copy-start(f32[16,60,16,128]{3,2,1,0:T(8,128)} %tracers_hbm.1) | copy-start | bytes 23592964
  3.9 1.2 %copy-start.1 = (f32[2,60,16,128]{3,2,1,0:T(8,128)S(1)}, f32[2,60,16,128]{3,2,1,0:T(8,128)}, u32[]{:S(2)}) copy-start(f32[2,60,16,128]{3,2,1,0:T(8,128)} %wind_hbm.1) | copy-start | bytes 2949124
  5.1 0.8 copy-start.2
  5.9 0.8 copy-start.3
  6.7 0.7 copy-start.4
  7.4 0.7 copy-start.5
  8.1 0.7 copy-start.6
  8.8 0.7 copy-start.7
where the time goes:
time: 89.1 us; the launch traced here: 88.3 us
  Pallas kernels  75 us (84%)
  local copies, waits for them, and re-layouts  12.7 us (14%)
    pallas_call x1, Pallas kernels, on_device(): pl.pallas_call(functools.partial(kernel, sizes + (chunk,)), out_shape=(ja...  75 us
    unnamed x18, local copies, waits for them, and re-layouts  12.7 us

commit v1 on v0

--- a/solution.py
+++ b/solution.py
@@ -8,6 +8,7 @@
 from jax.sharding import PartitionSpec as P
 
 SWEEPS = 3
+FIRST_LAG, SECOND_LAG = 2, 4
 MESH = pl.DeviceIdType.MESH
 UP, DOWN, RIGHT, LEFT = range(4)
 
@@ -34,6 +35,7 @@
     out_hbm,
     head_out_hbm,
     q,
+    middle,
     wind,
     row_send,
     row_recv,
@@ -98,10 +100,8 @@
         part = pl.ds(c * chunk, chunk)
         return pltpu.make_async_copy(q.at[:, part], out_hbm.at[:, part], store_sem.at[c])
 
-    @pl.loop(0, chunks)
-    def _(c):
-        for copy in load(c):
-            copy.start()
+    for copy in load(0):
+        copy.start()
 
     soil_loads = [
         pltpu.make_async_copy(source, target, soil_sem.at[place])
@@ -125,21 +125,22 @@
         def _(device=device):
             pl.semaphore_signal(barrier, inc=1, device_id=device, device_id_type=MESH)
 
+    @pl.loop(1, chunks)
+    def _(c):
+        for copy in load(c):
+            copy.start()
+
     pl.semaphore_wait(barrier, sum(there.astype(jnp.int32) for there, _ in greeted))
-
-    for way in range(4):
-        place = row_recv if way < 2 else col_recv
-
-        @pl.when(jnp.logical_not(gets[way]))
-        def _(place=place, way=way):
-            place[:, way % 2] = jnp.zeros_like(place[:, way % 2])
 
     def transfer(c, turn, way):
         part = pl.ds(c * chunk, chunk)
-        source, target = (row_send, row_recv) if way < 2 else (col_send, col_recv)
+        if way < 2:
+            source, target = row_send.at[turn, way, part], row_recv.at[turn, way, part]
+        else:
+            source, target = col_send.at[turn, part], col_recv.at[turn, way - 2, part]
         return pltpu.make_async_remote_copy(
-            src_ref=source.at[turn, way % 2, part],
-            dst_ref=target.at[turn, way % 2, part],
+            src_ref=source,
+            dst_ref=target,
             send_sem=send_sem.at[turn, way, c],
             recv_sem=recv_sem.at[turn, way, c],
             device_id=targets[way],
@@ -161,74 +162,97 @@
                 transfer(c, turn, way).wait_recv()
 
     lane = lax.broadcasted_iota(jnp.int32, (rows, cols), 1)
-    row = lax.broadcasted_iota(jnp.int32, (rows, cols), 0)
+
+    even = lax.rem(lane, 2) == 0
 
     def winds(level):
         u, v = wind[0, level], wind[1, level]
         return jnp.maximum(u, 0.0), jnp.minimum(u, 0.0), jnp.maximum(v, 0.0), jnp.minimum(v, 0.0)
 
-    def pack(level, turn, kind, field, parts, packed):
+    def pack(level, turn, kind, field, parts, edge_wind, packed):
+        u_pos, u_neg = parts[:2]
+        last, first = slice(rows - 1, rows), slice(0, 1)
+        row_send[turn, UP, level, kind : kind + 1] = u_pos[last] * field[last]
+        row_send[turn, DOWN, level, kind : kind + 1] = u_neg[first] * field[first]
+        part = edge_wind * field
+        if kind > 0:
+            part = pltpu.roll(part, 2 * kind, 1)
+        return packed + part
+
+    def edge_of(parts):
+        return jnp.where(lane == cols - 1, parts[2], jnp.where(lane == 0, parts[3], 0.0))
+
+    def blank():
+        return jnp.zeros((rows, cols), jnp.float32)
+
+    def side_halo(level, turn):
+        left = pltpu.roll(col_recv[turn, 0, level], 1, 1)
+        right = pltpu.roll(col_recv[turn, 1, level], cols - 1, 1)
+        return jnp.where(even, left, right)
+
+    def keep_of(parts):
         u_pos, u_neg, v_pos, v_neg = parts
-        right, left = packed
-        row_send[turn, UP, level, kind : kind + 1] = (u_pos * field)[rows - 1 : rows]
-        row_send[turn, DOWN, level, kind : kind + 1] = (u_neg * field)[0:1]
-        right = jnp.where(
-            lane == kind, pltpu.roll(v_pos * field, (kind + 1) % cols, 1), right
-        )
-        left_part = v_neg * field
+        return (1.0 - (u_pos - u_neg)) - (v_pos - v_neg)
+
+    blocks = rows // 8
+    row8 = lax.broadcasted_iota(jnp.int32, (8, cols), 0)
+
+    def advance(level, turn, kind, field, parts, keep, sides):
+        u_pos, u_neg, v_pos, v_neg = parts
+        plus, minus = u_pos * field, u_neg * field
+        plus = [pltpu.roll(plus[8 * b : 8 * b + 8], 1, 0) for b in range(blocks)]
+        minus = [pltpu.roll(minus[8 * b : 8 * b + 8], 7, 0) for b in range(blocks)]
+        below = [row_recv[turn, UP, level, kind : kind + 1]] + plus
+        above = minus + [row_recv[turn, DOWN, level, kind : kind + 1]]
+        inflow = jnp.concatenate(
+            [
+                jnp.where(row8 == 0, below[b], plus[b])
+                - jnp.where(row8 == 7, above[b + 1], minus[b])
+                for b in range(blocks)
+            ],
+            axis=0,
+        )
         if kind > 0:
-            left_part = pltpu.roll(left_part, kind, 1)
-        left = jnp.where(lane == kind, left_part, left)
-        return right, left
-
-    def pack_done(level, turn, packed):
-        col_send[turn, 0, level] = packed[0]
-        col_send[turn, 1, level] = packed[1]
-
-    def blank():
-        return (jnp.zeros((rows, cols), jnp.float32),) * 2
-
-    def advance(level, turn, kind, parts):
-        u_pos, u_neg, v_pos, v_neg = parts
-        field = q[kind, level]
-        plus, minus = u_pos * field, u_neg * field
-        above = row_recv[turn, DOWN, level, kind : kind + 1]
-        below = row_recv[turn, UP, level, kind : kind + 1]
-        face = plus + jnp.where(row == rows - 1, above, pltpu.roll(minus, rows - 1, 0))
-        face_before = jnp.where(row == 0, below + minus, pltpu.roll(face, 1, 0))
-        plus, minus = v_pos * field, v_neg * field
-        from_left = col_recv[turn, 0, level]
-        if kind > 0:
-            from_left = pltpu.roll(from_left, cols - kind, 1)
-        from_right = pltpu.roll(col_recv[turn, 1, level], cols - 1 - kind, 1)
-        side = plus + jnp.where(lane == cols - 1, from_right, pltpu.roll(minus, cols - 1, 1))
-        side_before = jnp.where(lane == 0, from_left, pltpu.roll(plus, 1, 1)) + minus
-        return field - (face - face_before) - (side - side_before)
+            sides = pltpu.roll(sides, cols - 2 * kind, 1)
+        right = jnp.where(lane == cols - 1, sides, pltpu.roll(v_neg * field, cols - 1, 1))
+        left = jnp.where(lane == 0, sides, pltpu.roll(v_pos * field, 1, 1))
+        return keep * field + inflow + (left - right)
+
+    def close_ends():
+        for way in range(4):
+            place = row_recv if way < 2 else col_recv
+
+            @pl.when(jnp.logical_not(gets[way]))
+            def _(place=place, way=way):
+                place[:, way % 2] = jnp.zeros_like(place[:, way % 2])
 
     def first_edges(c):
         @pl.loop(c * chunk, (c + 1) * chunk)
         def _(level):
             parts, packed = winds(level), blank()
+            edge_wind = edge_of(parts)
             for kind in range(species):
-                packed = pack(level, 0, kind, q[kind, level], parts, packed)
-            pack_done(level, 0, packed)
+                packed = pack(level, 0, kind, q[kind, level], parts, edge_wind, packed)
+            col_send[0, level] = packed
 
     def first_step(c):
         @pl.loop(c * chunk, (c + 1) * chunk)
         def _(level):
             parts, packed = winds(level), blank()
+            edge_wind, keep, sides = edge_of(parts), keep_of(parts), side_halo(level, 0)
             for kind in range(species):
-                field = advance(level, 0, kind, parts)
-                packed = pack(level, 1, kind, field, parts, packed)
-                q[kind, level] = field
-            pack_done(level, 1, packed)
+                field = advance(level, 0, kind, q[kind, level], parts, keep, sides)
+                packed = pack(level, 1, kind, field, parts, edge_wind, packed)
+                middle[kind, level] = field
+            col_send[1, level] = packed
 
     def second_step(c):
         @pl.loop(c * chunk, (c + 1) * chunk)
         def _(level):
-            parts = winds(level)
+            parts, sides = winds(level), side_halo(level, 1)
+            keep = keep_of(parts)
             for kind in range(species):
-                q[kind, level] = advance(level, 1, kind, parts)
+                q[kind, level] = advance(level, 1, kind, middle[kind, level], parts, keep, sides)
 
     edge_sends = (along < n_along - 1, along > 0, mp >= 0)
     edge_gets = (along > 0, along < n_along - 1, mp >= 0)
@@ -369,7 +393,7 @@
 
     head_store = pltpu.make_async_copy(iterate, head_out_hbm, head_sem.at[0])
 
-    @pl.loop(0, chunks + 2)
+    @pl.loop(0, chunks + SECOND_LAG)
     def _(turn):
         @pl.when(turn < chunks)
         def _():
@@ -380,36 +404,37 @@
 
         @pl.when(turn == 0)
         def _():
+            close_ends()
             soil_start()
 
-        @pl.when(jnp.logical_and(turn >= 1, turn <= chunks))
-        def _():
-            arrive(turn - 1, 0)
-            first_step(turn - 1)
-            start(turn - 1, 1)
-
-        @pl.when(turn >= 2)
-        def _():
-            arrive(turn - 2, 1)
-            second_step(turn - 2)
-            store(turn - 2).start()
-
-        @pl.when(turn == 2)
+        @pl.when(jnp.logical_and(turn >= FIRST_LAG, turn < chunks + FIRST_LAG))
+        def _():
+            arrive(turn - FIRST_LAG, 0)
+            first_step(turn - FIRST_LAG)
+            start(turn - FIRST_LAG, 1)
+
+        @pl.when(turn >= SECOND_LAG)
+        def _():
+            arrive(turn - SECOND_LAG, 1)
+            second_step(turn - SECOND_LAG)
+            store(turn - SECOND_LAG).start()
+
+        @pl.when(turn == SECOND_LAG)
         def _():
             surface_start()
 
-        @pl.when(turn == 4)
+        @pl.when(turn == SECOND_LAG + 2)
         def _():
             surface_wait()
             soil_sweep(0)
             soil_edges(1)
 
-        @pl.when(turn == 6)
+        @pl.when(turn == SECOND_LAG + 4)
         def _():
             soil_sweep(1)
             soil_edges(2)
 
-        @pl.when(turn == 8)
+        @pl.when(turn == SECOND_LAG + 6)
         def _():
             soil_sweep(2)
             head_store.start()
@@ -455,10 +480,11 @@
         out_specs=(anywhere, anywhere),
         scratch_shapes=[
             pltpu.VMEM(tracers.shape, f32),
+            pltpu.VMEM(tracers.shape, f32),
             pltpu.VMEM(wind.shape, f32),
             pltpu.VMEM((2, 2, levels, species, cols), f32),
             pltpu.VMEM((2, 2, levels, species, cols), f32),
-            pltpu.VMEM((2, 2, levels, rows, cols), f32),
+            pltpu.VMEM((2, levels, rows, cols), f32),
             pltpu.VMEM((2, 2, levels, rows, cols), f32),
             pltpu.VMEM(soil, f32),
             pltpu.VMEM(soil, f32),
@@ -485,9 +511,9 @@
             pltpu.SemaphoreType.DMA((1,)),
         ],
         compiler_params=pltpu.CompilerParams(
-            collective_id=0, has_side_effects=True, vmem_limit_bytes=28 * 1024 * 1024
+            collective_id=0, has_side_effects=True, vmem_limit_bytes=36 * 1024 * 1024
         ),
-    )(*arguments)
+    )(*[pltpu.with_memory_space_constraint(a, pltpu.HBM) for a in arguments])
 
 
 def solution(mesh):

time: 89.1 us -> 59.4 us (0.67)
  Pallas kernels: 75 us -> 54.7 us
  local copies, waits for them, and re-layouts: 12.7 us -> 3.85 us
    pallas_call x1, Pallas kernels: 75 us -> 54.7 us  [on_device(): pl.pallas_call(functools.partial(kernel, sizes + (chunk,)), out_shape=(ja...]
    unnamed x18 -> x2, local copies, waits for them, and re-layouts: 12.7 us -> 3.85 us
where the time goes in v1:
time: 59.4 us; the launch traced here: 59.2 us
  Pallas kernels  54.7 us (92%)
  local copies, waits for them, and re-layouts  3.85 us (6%)
  between operations  0.64 us (1%)
    pallas_call x1, Pallas kernels, on_device(): pl.pallas_call(functools.partial(kernel, sizes + (chunk,)), out_shape=(ja...  54.7 us
    unnamed x2, local copies, waits for them, and re-layouts  3.85 us

profile of v1, /device:TPU:16, one launch (start us, length us, event | category | flops | bytes accessed | tf_op | source)
XLA Modules:
  0.0 59.2 jit_solution(17301737774813488610)
XLA Ops:
  0.6 54.7 %shard_map.95 = (f32[16,60,16,128]{3,2,1,0:T(8,128)S(1)}, f32[8,8,256]{2,1,0:T(8,128)S(1)}) custom-call(f32[16,60,16,128]{3,2,1,0:T(8,128)} %tracers_hbm.1, f32[2,60,16,128]{3,2,1,0:T(8,128)} %wind_hbm.1, f32[8,8,256]{2,1,0:T(8,128)} %head_hbm.1, f32[8,8,256]{2,1,0:T(8,128)} %storage_hbm.1, s32[8,256]{1,0:T(8,128)} %type_hbm.1, s32[8,256]{1,0:T(8,128)} %mask_hbm.1, ...), custom_call_target="tpu_custom_call" | custom-call | tf_op jit(solution)/shard_map/pallas_call | solution.py:473
  55.4 3.2 %copy.12 = f32[16,60,16,128]{3,2,1,0:T(8,128)} copy(f32[16,60,16,128]{3,2,1,0:T(8,128)S(1)} %get-tuple-element.4) | data formatting | bytes 15728640
  58.6 0.6 %copy.13 = f32[8,8,256]{2,1,0:T(8,128)} copy(f32[8,8,256]{2,1,0:T(8,128)S(1)} %get-tuple-element.5) | data formatting | bytes 131072

commit v2 on v1

--- a/solution.py
+++ b/solution.py
@@ -30,8 +30,8 @@
     storage_hbm,
     type_hbm,
     mask_hbm,
-    cond_table,
-    exp_table,
+    cond_table_hbm,
+    exp_table_hbm,
     out_hbm,
     head_out_hbm,
     q,
@@ -41,6 +41,8 @@
     row_recv,
     col_send,
     col_recv,
+    cond_table,
+    exp_table,
     head,
     storage,
     soil_type,
@@ -106,7 +108,14 @@
     soil_loads = [
         pltpu.make_async_copy(source, target, soil_sem.at[place])
         for place, (source, target) in enumerate(
-            ((head_hbm, head), (storage_hbm, storage), (type_hbm, soil_type), (mask_hbm, mask))
+            (
+                (head_hbm, head),
+                (storage_hbm, storage),
+                (type_hbm, soil_type),
+                (mask_hbm, mask),
+                (cond_table_hbm, cond_table),
+                (exp_table_hbm, exp_table),
+            )
         )
     ]
     for copy in soil_loads:
@@ -402,7 +411,7 @@
             first_edges(turn)
             start(turn, 0)
 
-        @pl.when(turn == 0)
+        @pl.when(turn == 1)
         def _():
             close_ends()
             soil_start()
@@ -468,7 +477,6 @@
     chunks = levels // chunk
     f32 = jnp.float32
     anywhere = pl.BlockSpec(memory_space=pl.ANY)
-    scalars = pl.BlockSpec(memory_space=pltpu.SMEM)
     soil = (layers, soil_rows, soil_cols)
     return pl.pallas_call(
         functools.partial(kernel, sizes + (chunk,)),
@@ -476,7 +484,7 @@
             jax.ShapeDtypeStruct(tracers.shape, f32),
             jax.ShapeDtypeStruct(head.shape, f32),
         ),
-        in_specs=[pl.BlockSpec(memory_space=pltpu.HBM)] * 6 + [scalars] * 2,
+        in_specs=[pl.BlockSpec(memory_space=pltpu.HBM)] * 8,
         out_specs=(anywhere, anywhere),
         scratch_shapes=[
             pltpu.VMEM(tracers.shape, f32),
@@ -486,6 +494,8 @@
             pltpu.VMEM((2, 2, levels, species, cols), f32),
             pltpu.VMEM((2, levels, rows, cols), f32),
             pltpu.VMEM((2, 2, levels, rows, cols), f32),
+            pltpu.SMEM(arguments[6].shape, f32),
+            pltpu.SMEM(arguments[7].shape, f32),
             pltpu.VMEM(soil, f32),
             pltpu.VMEM(soil, f32),
             pltpu.VMEM(soil[1:], jnp.int32),
@@ -501,7 +511,7 @@
             pltpu.VMEM((SWEEPS, 2, layers, soil_rows, soil_cols // 2), f32),
             pltpu.VMEM((SWEEPS, 2, layers, soil_rows, soil_cols // 2), f32),
             pltpu.SemaphoreType.DMA((2, chunks)),
-            pltpu.SemaphoreType.DMA((4,)),
+            pltpu.SemaphoreType.DMA((6,)),
             pltpu.SemaphoreType.DMA((chunks,)),
             pltpu.SemaphoreType.DMA((2, 4, chunks)),
             pltpu.SemaphoreType.DMA((2, 4, chunks)),

time: 59.4 us -> 58.7 us (0.988)
  Pallas kernels: 54.7 us -> 54.1 us
    pallas_call x1, Pallas kernels: 54.7 us -> 54.1 us  [on_device(): pl.pallas_call(functools.partial(kernel, sizes + (chunk,)), out_shape=(ja...]
where the time goes in v2:
time: 58.7 us; the launch traced here: 58.6 us
  Pallas kernels  54.1 us (92%)
  local copies, waits for them, and re-layouts  3.85 us (7%)
  between operations  0.64 us (1%)
    pallas_call x1, Pallas kernels, on_device(): pl.pallas_call(functools.partial(kernel, sizes + (chunk,)), out_shape=(ja...  54.1 us
    unnamed x2, local copies, waits for them, and re-layouts  3.85 us

profile of v2, /device:TPU:16, one launch (start us, length us, event | category | flops | bytes accessed | tf_op | source)
XLA Modules:
  0.0 58.6 jit_solution(9927349588270501517)
XLA Ops:
  0.6 54.1 %shard_map.95 = (f32[16,60,16,128]{3,2,1,0:T(8,128)S(1)}, f32[8,8,256]{2,1,0:T(8,128)S(1)}) custom-call(f32[16,60,16,128]{3,2,1,0:T(8,128)} %tracers_hbm.1, f32[2,60,16,128]{3,2,1,0:T(8,128)} %wind_hbm.1, f32[8,8,256]{2,1,0:T(8,128)} %head_hbm.1, f32[8,8,256]{2,1,0:T(8,128)} %storage_hbm.1, s32[8,256]{1,0:T(8,128)} %type_hbm.1, s32[8,256]{1,0:T(8,128)} %mask_hbm.1, ...), custom_call_target="tpu_custom_call" | custom-call | tf_op jit(solution)/shard_map/pallas_call | solution.py:481
  54.7 3.2 %copy.12 = f32[16,60,16,128]{3,2,1,0:T(8,128)} copy(f32[16,60,16,128]{3,2,1,0:T(8,128)S(1)} %get-tuple-element.4) | data formatting | bytes 15728640
  58.0 0.6 %copy.13 = f32[8,8,256]{2,1,0:T(8,128)} copy(f32[8,8,256]{2,1,0:T(8,128)S(1)} %get-tuple-element.5) | data formatting | bytes 131072
